TPU v7x, 32 devices: a whole 2x2x4 slice. The times are simulated.
32 devices in a mesh: dp: 16 (over z, y, x), section: 2 (over core).
Axes of the slice: x: 2, y: 2, z: 4, core: 2. Of those that a mesh axis runs over, the one named last changes fastest.
Arguments:
- patches: bfloat16 [8192, 768], P('dp'), may hold values from -4 to 4
- recon_cot: bfloat16 [8192, 768], P('dp'), may hold values from -6 to 6
- lengths: int32 [32, 4], P('dp'), may hold values from 1 to 128, 256 in all within a row
- codebook: bfloat16 [4096, 768], P(('dp', 'section')), may hold values from -4 to 4
- w_qkv: bfloat16 [2, 768, 2304], P('section'), may hold values from -0.21875 to 0.21875
- w_out: bfloat16 [2, 768, 768], P('section'), may hold values from -0.625 to 0.625
- w_up: bfloat16 [2, 768, 3072], P('section'), may hold values from -0.21875 to 0.21875
- w_down: bfloat16 [2, 3072, 768], P('section'), may hold values from -0.109375 to 0.109375
- norm_gain: float32 [2, 2, 768], P('section'), may hold values from 0.1 to 1.9
- norm_bias: float32 [2, 2, 768], P('section'), may hold values from -3 to 3
- bias_out: float32 [2, 2, 768], P('section'), may hold values from -3 to 3
- bias_up: float32 [2, 3072], P('section'), may hold values from -3 to 3
Outputs:
- ends: float32 [2, 8192, 768], P('section', 'dp')
- codes: float32 [8192], P('dp')
- grad_qkv: float32 [2, 768, 2304], P('section', 'dp')
- grad_out: float32 [2, 768, 768], P('section', 'dp')
- grad_up: float32 [2, 768, 3072], P('section', 'dp')
- grad_down: float32 [2, 3072, 768], P('section', 'dp')
- grad_gain: float32 [2, 2, 768], P('section', None, 'dp')
- grad_nbias: float32 [2, 2, 768], P('section', None, 'dp')
- grad_bout: float32 [2, 2, 768], P('section', None, 'dp')
- grad_bup: float32 [2, 3072], P('section', 'dp')
Inputs may be any that keep to these rules, and one draw needn't show every extreme that they name: In each row the 4 image lengths sum to 256, and the largest is exactly half of 256.
All inputs are finite; a program needn't handle non-finite values.
Results may differ from a plain program's by a relative error of at most 0.025.
Values may be sent and summed in bfloat16 or wider, within the bound.
No kernel may reach another device: no remote copies, remote signals or barrier semaphores. Data moves between devices by JAX's collectives and lax.ppermute only.
A program may use at most 256 MiB of HBM per device.

v0:
```python
from functools import partial

import jax
import jax.numpy as jnp
from jax import lax
from jax.sharding import PartitionSpec as P

D = 768
HEADS = 12
HD = 64


EPS = 1e-06
MASKED = -1e30


def passed_along(block, axis, distance):
    devices = range(lax.axis_size(axis))
    route = [(i - distance, i) for i in devices if i - distance in devices]
    return lax.ppermute(block, axis, route)


def merged(value, axis, join):
    pieces = jax.tree.map(lambda part: lax.all_gather(part, axis), value)
    head = jax.tree.map(lambda part: part[0], pieces)
    tail = jax.tree.map(lambda part: part[1:], pieces)
    subtotal, _ = lax.scan(lambda subtotal, section: (join(subtotal, section), None), head, tail)
    return subtotal


def image_mask(image_lens, row_count):
    limits = jnp.cumsum(image_lens)
    positions = jnp.arange(row_count, dtype=jnp.int32)
    idents = jnp.sum((positions[:, None] >= limits[None, :]).astype(jnp.int32), axis=1)
    return idents[:, None] == idents[None, :]


def norm_parts(values, gains, shifts):
    centre = values - jnp.mean(values, axis=-1, keepdims=True)
    inverse = lax.rsqrt(jnp.mean(centre * centre, axis=-1, keepdims=True) + EPS)
    unit_rows = centre * inverse
    return (unit_rows * gains + shifts, unit_rows, inverse)


def norm_back(grad_rows, unit_rows, inverse, gains):
    scaled = grad_rows * gains
    return inverse * (
        scaled
        - jnp.mean(scaled, axis=-1, keepdims=True)
        - unit_rows * jnp.mean(scaled * unit_rows, axis=-1, keepdims=True)
    )


def head_scores(query_heads, key_heads, same):
    scores = jnp.einsum(
        "qhd,khd->hqk", query_heads, key_heads, preferred_element_type=jnp.float32
    ) * HD ** (-0.5)
    return jnp.where(same[None], scores, MASKED)


def block_forward(inputs, same, weights):
    w_qkv, w_out, w_up, w_down, gains, shifts, bias_out, bias_up = weights
    row_count = inputs.shape[0]
    normed, unit_one, inv_one = norm_parts(inputs, gains[0], shifts[0])
    normed_low = normed.astype(jnp.bfloat16)
    packed = jnp.dot(normed_low, w_qkv, preferred_element_type=jnp.float32).astype(jnp.bfloat16)
    heads = packed.reshape(row_count, 3, HEADS, HD)
    scores = head_scores(heads[:, 0], heads[:, 1], same)
    highest = jnp.max(scores, axis=-1, keepdims=True)
    powers = jnp.exp(scores - highest)
    totals = jnp.sum(powers, axis=-1, keepdims=True)
    att_probs = powers / totals
    log_total = highest + jnp.log(totals)
    mixed_heads = jnp.einsum(
        "hqk,khd->qhd",
        att_probs.astype(jnp.bfloat16),
        heads[:, 2],
        preferred_element_type=jnp.float32,
    )
    mixed_heads = mixed_heads.reshape(row_count, HEADS * HD).astype(jnp.bfloat16)
    residual = (
        inputs + jnp.dot(mixed_heads, w_out, preferred_element_type=jnp.float32) + bias_out[0]
    )
    normed_two, unit_two, inv_two = norm_parts(residual, gains[1], shifts[1])
    normed_two_low = normed_two.astype(jnp.bfloat16)
    pre_act = jnp.dot(normed_two_low, w_up, preferred_element_type=jnp.float32) + bias_up
    active = jax.nn.gelu(pre_act, approximate=False).astype(jnp.bfloat16)
    output = residual + jnp.dot(active, w_down, preferred_element_type=jnp.float32) + bias_out[1]
    kept_state = (
        unit_one,
        inv_one,
        normed_low,
        packed,
        log_total,
        mixed_heads,
        unit_two,
        inv_two,
        normed_two_low,
        pre_act,
        active,
    )
    return (output, kept_state)


def block_backward(grad_rows, kept_state, same, weights):
    w_qkv, w_out, w_up, w_down, gains, shifts, bias_out, bias_up = weights
    (
        unit_one,
        inv_one,
        normed_low,
        packed,
        log_total,
        mixed_heads,
        unit_two,
        inv_two,
        normed_two_low,
        pre_act,
        active,
    ) = kept_state
    row_count = grad_rows.shape[0]
    grad_low = grad_rows.astype(jnp.bfloat16)
    grad_down = jnp.einsum("rf,rd->fd", active, grad_low, preferred_element_type=jnp.float32)
    d_active = jnp.einsum("rd,fd->rf", grad_low, w_down, preferred_element_type=jnp.float32)
    _, gelu_pull = jax.vjp(partial(jax.nn.gelu, approximate=False), pre_act)
    d_pre = gelu_pull(d_active)[0].astype(jnp.bfloat16)
    grad_up = jnp.einsum("rd,rf->df", normed_two_low, d_pre, preferred_element_type=jnp.float32)
    grad_bias_up = jnp.sum(d_pre.astype(jnp.float32), axis=0)
    d_normed_two = jnp.einsum("rf,df->rd", d_pre, w_up, preferred_element_type=jnp.float32)
    gain_two = jnp.sum(d_normed_two * unit_two, axis=0)
    shift_two = jnp.sum(d_normed_two, axis=0)
    grad_resid = grad_rows + norm_back(d_normed_two, unit_two, inv_two, gains[1])
    resid_low = grad_resid.astype(jnp.bfloat16)
    grad_outw = jnp.einsum("re,rd->ed", mixed_heads, resid_low, preferred_element_type=jnp.float32)
    d_mixed = jnp.einsum("rd,ed->re", resid_low, w_out, preferred_element_type=jnp.float32)
    d_mixed = d_mixed.astype(jnp.bfloat16).reshape(row_count, HEADS, HD)
    heads = packed.reshape(row_count, 3, HEADS, HD)
    query_heads = heads[:, 0]
    key_heads = heads[:, 1]
    value_heads = heads[:, 2]
    att_probs = jnp.exp(head_scores(query_heads, key_heads, same) - log_total)
    d_probs = jnp.einsum("qhd,khd->hqk", d_mixed, value_heads, preferred_element_type=jnp.float32)
    d_value = jnp.einsum(
        "hqk,qhd->khd", att_probs.astype(jnp.bfloat16), d_mixed, preferred_element_type=jnp.float32
    )
    d_scores = att_probs * (d_probs - jnp.sum(d_probs * att_probs, axis=-1, keepdims=True))
    d_scores = d_scores.astype(jnp.bfloat16)
    d_query = jnp.einsum(
        "hqk,khd->qhd", d_scores, key_heads, preferred_element_type=jnp.float32
    ) * HD ** (-0.5)
    d_key = jnp.einsum(
        "hqk,qhd->khd", d_scores, query_heads, preferred_element_type=jnp.float32
    ) * HD ** (-0.5)
    d_packed = jnp.stack((d_query, d_key, d_value), axis=1).reshape(row_count, 3 * HEADS * HD)
    d_packed = d_packed.astype(jnp.bfloat16)
    grad_qkvw = jnp.einsum("rd,re->de", normed_low, d_packed, preferred_element_type=jnp.float32)
    d_normed = jnp.einsum("re,de->rd", d_packed, w_qkv, preferred_element_type=jnp.float32)
    gain_one = jnp.sum(d_normed * unit_one, axis=0)
    shift_one = jnp.sum(d_normed, axis=0)
    grad_input = grad_resid + norm_back(d_normed, unit_one, inv_one, gains[0])
    grad_parts = (
        grad_qkvw,
        grad_outw,
        grad_up,
        grad_down,
        jnp.stack((gain_one, gain_two)),
        jnp.stack((shift_one, shift_two)),
        jnp.stack((jnp.sum(grad_resid, axis=0), jnp.sum(grad_rows, axis=0))),
        grad_bias_up,
    )
    return (grad_input, grad_parts)


def soft_step(hidden_low, score_scale):

    def fold_rows(running, code_piece, offset):
        highest, totals, summed = running
        scores = (
            jnp.einsum("rd,vd->rv", hidden_low, code_piece, preferred_element_type=jnp.float32)
            * score_scale
        )
        new_high = jnp.maximum(highest, jnp.max(scores, axis=-1, keepdims=True))
        powers = jnp.exp(scores - new_high)
        high_part = powers.astype(jnp.bfloat16)
        low_part = (powers - high_part.astype(jnp.float32)).astype(jnp.bfloat16)
        gained = jnp.dot(high_part, code_piece, preferred_element_type=jnp.float32) + jnp.dot(
            low_part, code_piece, preferred_element_type=jnp.float32
        )
        return (new_high, jnp.sum(powers, axis=-1, keepdims=True), gained)

    return fold_rows


def back_step(hidden_low, log_total, grad_low, inner_prod, score_scale):

    def fold_rows(running, code_piece, offset):
        scores = (
            jnp.einsum("rd,vd->rv", hidden_low, code_piece, preferred_element_type=jnp.float32)
            * score_scale
        )
        code_probs = jnp.exp(scores - log_total)
        d_probs = jnp.einsum("rd,vd->rv", grad_low, code_piece, preferred_element_type=jnp.float32)
        d_scores = (code_probs * (d_probs - inner_prod)).astype(jnp.bfloat16)
        return jnp.dot(d_scores, code_piece, preferred_element_type=jnp.float32) * score_scale

    return fold_rows


def merge_soft(left_part, right_part):
    highest = jnp.maximum(left_part[0], right_part[0])
    left_factor = jnp.exp(left_part[0] - highest)
    right_factor = jnp.exp(right_part[0] - highest)
    return (
        highest,
        left_part[1] * left_factor + right_part[1] * right_factor,
        left_part[2] * left_factor + right_part[2] * right_factor,
    )


def fold_forward(codebook, fold_rows, initial):
    return fold_rows(initial, lax.all_gather(codebook, "dp", axis=0, tiled=True), jnp.int32(0))


def fold_backward(codebook, fold_rows, initial):
    return fold_rows(initial, lax.all_gather(codebook, "dp", axis=0, tiled=True), jnp.int32(0))


def per_device(
    patches,
    recon_cot,
    lengths,
    codebook,
    w_qkv,
    w_out,
    w_up,
    w_down,
    norm_gain,
    norm_bias,
    bias_out,
    bias_up,
):
    on_first = lax.axis_index("section") == 0
    micro_count = lengths.shape[0]
    row_count = patches.shape[0] // micro_count
    score_scale = D ** (-0.5)
    weights = (
        w_qkv[0],
        w_out[0],
        w_up[0],
        w_down[0],
        norm_gain[0],
        norm_bias[0],
        bias_out[0],
        bias_up[0],
    )
    masks = [image_mask(lengths[number], row_count) for number in range(micro_count)]
    inputs = patches.astype(jnp.float32).reshape(micro_count, row_count, D)
    targets = recon_cot.astype(jnp.float32).reshape(micro_count, row_count, D)
    blank = jnp.zeros((row_count, D), jnp.float32)
    codes_state = []
    kept_steps = []
    recons = []
    units = []
    for step_index in range(micro_count + 1):
        enc_in = inputs[step_index] if step_index < micro_count else blank
        dec_in = units[step_index - 1] if step_index > 0 else blank
        enc_mask = masks[min(step_index, micro_count - 1)]
        dec_mask = masks[max(step_index - 1, 0)]
        block_in = jnp.where(on_first, enc_in, dec_in)
        block_mask = jnp.where(on_first, enc_mask, dec_mask)
        output, kept_state = block_forward(block_in, block_mask, weights)
        kept_steps.append((kept_state, block_mask))
        if step_index > 0:
            recons.append(output)
        if step_index < micro_count:
            sent_rows = output.astype(jnp.bfloat16)
            received = passed_along(sent_rows, "section", 1)
            hidden_low = jnp.where(on_first, sent_rows, received)
            initial = (
                jnp.full((row_count, 1), MASKED, jnp.float32),
                jnp.zeros((row_count, 1), jnp.float32),
                blank,
            )
            partial_soft = fold_forward(codebook, soft_step(hidden_low, score_scale), initial)
            highest, totals, summed = merged(partial_soft, "section", merge_soft)
            log_total = highest + jnp.log(totals)
            mean_code = summed / totals
            inverse = lax.rsqrt(jnp.mean(mean_code * mean_code, axis=-1, keepdims=True) + EPS)
            unit_code = mean_code * inverse
            units.append(unit_code)
            codes_state.append((hidden_low, log_total, mean_code, unit_code, inverse))
    pending = blank
    patch_grads = [blank] * micro_count
    grad_totals = None
    for back_index in range(micro_count + 1):
        fwd_index = micro_count - back_index
        dec_grad = targets[micro_count - 1 - back_index] if back_index < micro_count else blank
        grad_rows = jnp.where(on_first, pending, dec_grad)
        kept_state, block_mask = kept_steps[fwd_index]
        grad_input, grad_parts = block_backward(grad_rows, kept_state, block_mask, weights)
        if grad_totals is None:
            grad_totals = grad_parts
        else:
            grad_totals = jax.tree.map(jnp.add, grad_totals, grad_parts)
        if back_index > 0:
            patch_grads[fwd_index] = grad_input
        if back_index < micro_count:
            hidden_low, log_total, mean_code, unit_code, inverse = codes_state[
                micro_count - 1 - back_index
            ]
            grad_code = inverse * (
                grad_input - unit_code * jnp.mean(grad_input * unit_code, axis=-1, keepdims=True)
            )
            own_low = grad_code.astype(jnp.bfloat16)
            got_low = passed_along(own_low, "section", -1)
            code_grad_low = jnp.where(on_first, got_low, own_low)
            inner_prod = jnp.sum(
                code_grad_low.astype(jnp.float32) * mean_code, axis=-1, keepdims=True
            )
            half_grad = fold_backward(
                codebook,
                back_step(hidden_low, log_total, code_grad_low, inner_prod, score_scale),
                blank,
            )
            other_half = passed_along(half_grad.astype(jnp.bfloat16), "section", -1).astype(
                half_grad.dtype
            )
            pending = half_grad + other_half
    sum_qkv, sum_out, sum_up, sum_down, sum_gain, sum_shift, sum_bout, sum_bup = grad_totals
    summed_grads = (
        lax.psum_scatter(sum_qkv, "dp", scatter_dimension=0, tiled=True),
        lax.psum_scatter(sum_out, "dp", scatter_dimension=0, tiled=True),
        lax.psum_scatter(sum_up, "dp", scatter_dimension=0, tiled=True),
        lax.psum_scatter(sum_down, "dp", scatter_dimension=0, tiled=True),
        lax.psum_scatter(sum_gain, "dp", scatter_dimension=1, tiled=True),
        lax.psum_scatter(sum_shift, "dp", scatter_dimension=1, tiled=True),
        lax.psum_scatter(sum_bout, "dp", scatter_dimension=1, tiled=True),
        lax.psum_scatter(sum_bup, "dp", scatter_dimension=0, tiled=True),
    )
    ends = jnp.where(
        on_first, jnp.concatenate(patch_grads, axis=0), jnp.concatenate(recons, axis=0)
    )[None]
    codes = jnp.concatenate([state[1][:, 0] for state in codes_state], axis=0)
    return (
        ends,
        codes,
        summed_grads[0][None],
        summed_grads[1][None],
        summed_grads[2][None],
        summed_grads[3][None],
        summed_grads[4][None],
        summed_grads[5][None],
        summed_grads[6][None],
        summed_grads[7][None],
    )


def solution(mesh):
    placed = (
        P("dp", None),
        P("dp", None),
        P("dp", None),
        P(("dp", "section"), None),
        P("section", None, None),
        P("section", None, None),
        P("section", None, None),
        P("section", None, None),
        P("section", None, None),
        P("section", None, None),
        P("section", None, None),
        P("section", None),
    )
    return jax.shard_map(
        per_device,
        mesh=mesh,
        in_specs=placed,
        out_specs=(
            P("section", "dp", None),
            P("dp"),
            P("section", "dp", None),
            P("section", "dp", None),
            P("section", "dp", None),
            P("section", "dp", None),
            P("section", None, "dp"),
            P("section", None, "dp"),
            P("section", None, "dp"),
            P("section", "dp"),
        ),
        check_vma=False,
    )
```

profile of v0, /device:TPU:0, one launch (start us, length us, event | category | flops | bytes accessed | tf_op | source)
XLA Modules:
  0.0 1307.1 jit_solution(6374333337774689229)
XLA Ops:
  8.0 2.7 convert_element_type.258
  14.1 3.3 convolution_convert_fusion.2
  17.5 2.4 copy.85
  28.5 3.6 fusion.137
  33.2 11.0 multiply_convert_fusion.5
  45.7 3.2 collective-permute-start
  49.5 32.1 %all-gather.14.cloned.1.call-done = bf16[2048,768]{1,0:T(8,128)(2,1)} async-done(((bf16[128,768]{1,0:T(8,128)(2,1)}), bf16[2048,768]{1,0:T(8,128)(2,1)}) %all-gather.14.cloned.1.call-update) | async-done | bytes 3145744 | tf_op jit(solution)/shard_map/all_gather | solution.py:224
  81.7 3.3 fusion.224
  86.3 1.9 fusion.105
  88.3 2.0 fusion.73
  92.1 2.4 all-gather.6
  102.2 2.2 convolution_convert_fusion.1
  104.4 2.4 copy.87
  109.1 3.6 fusion.136
  113.7 11.1 multiply_convert_fusion.4
  124.9 2.3 fusion.227
  127.2 2.1 collective-permute-start.1
  133.1 1.9 fusion.108
  135.1 2.5 convert_element_type.285
  138.7 1.8 all-gather.9
  140.6 1.9 all-gather.8
  143.1 3.2 all-gather.18.cloned.1.call-done
  146.3 1.8 multiply_reduce_fusion.21
  151.3 2.2 convolution_convert_fusion
  153.5 2.4 copy.89
  155.9 1.9 fusion.229
  162.2 9.5 multiply_convert_fusion
  171.8 2.8 convert_reduce_fusion.2
  174.6 2.2 multiply_reduce_fusion.7
  179.9 1.9 copy.91
  181.9 3.1 multiply_reduce_fusion.2
  188.4 2.0 multiply_reduce_fusion.8
  192.5 2.3 collective-permute-done.2
  195.6 6.6 fusion.231
  206.0 2.1 fusion.211
  208.1 7.2 convert_reduce_fusion.1
  215.3 5.2 multiply_reduce_fusion.5
  223.6 1.9 copy.95
  225.6 3.1 multiply_reduce_fusion.1
  232.1 1.9 multiply_reduce_fusion.6
  239.3 6.6 fusion.232
  247.6 3.3 fusion.194
  258.1 1.9 fusion.188
  260.1 5.4 convert_reduce_fusion
  265.6 2.2 multiply_reduce_fusion.3
  270.9 1.9 copy.99
  272.8 3.1 multiply_reduce_fusion
  285.0 4.3 multiply_reduce_fusion.4
  297.2 4.6 add_add_fusion.3
  302.2 2.7 fusion.173
  306.7 4.3 add_add_fusion.2
  311.1 3.2 fusion.197
  315.8 5.1 add_add_fusion
  321.3 3.4 fusion.207
  326.4 6.8 add_add_fusion.1
  335.8 5.4 fusion.129
  341.8 77.0 %all-reduce = f32[3072]{0:T(1024)} all-reduce(f32[3072]{0:T(1024)} %add_add_fusion.4), channel_id=15, replica_groups=mesh['dp'=16,'section'=2] {'dp'}, use_global_device_ids=true, to_apply=%region_75.76.clone | all-reduce | flops 3072 | bytes 24576
  421.6 1.9 add_bitcast_fusion
  426.3 107.0 %reduce-scatter.24.cloned.1.call-done = f32[48,2]{1,0:T(8,128)} async-done(((f32[768,2]{1,0:T(8,128)}), f32[48,2]{1,0:T(8,128)}) %reduce-scatter.24.cloned.1.call-update) | async-done | bytes 400
  534.6 123.9 %reduce-scatter.22.cloned.1.call-done = f32[48,2]{1,0:T(8,128)} async-done(((f32[768,2]{1,0:T(8,128)}), f32[48,2]{1,0:T(8,128)}) %reduce-scatter.22.cloned.1.call-update) | async-done | bytes 400
  659.8 131.6 %reduce-scatter.16.cloned.1.call-done = f32[48,768]{1,0:T(8,128)} async-done(((f32[768,768]{1,0:T(8,128)}), f32[48,768]{1,0:T(8,128)}) %reduce-scatter.16.cloned.1.call-update) | async-done | bytes 147472 | tf_op jit(solution)/shard_map/reduce_scatter | solution.py:331
  791.4 155.5 %reduce-scatter.14.cloned.1.call-done = f32[48,2304]{1,0:T(8,128)} async-done(((f32[768,2304]{1,0:T(8,128)}), f32[48,2304]{1,0:T(8,128)}) %reduce-scatter.14.cloned.1.call-update) | async-done | bytes 442384 | tf_op jit(solution)/shard_map/reduce_scatter | solution.py:330
  946.9 176.1 %reduce-scatter.20.cloned.1.call-done = f32[192,768]{1,0:T(8,128)} async-done(((f32[3072,768]{1,0:T(8,128)}), f32[192,768]{1,0:T(8,128)}) %reduce-scatter.20.cloned.1.call-update) | async-done | bytes 589840 | tf_op jit(solution)/shard_map/reduce_scatter | solution.py:333
  1122.9 176.9 %reduce-scatter.18.cloned.1.call-done = f32[48,3072]{1,0:T(8,128)} async-done(((f32[768,3072]{1,0:T(8,128)}), f32[48,3072]{1,0:T(8,128)}) %reduce-scatter.18.cloned.1.call-update) | async-done | bytes 589840 | tf_op jit(solution)/shard_map/reduce_scatter | solution.py:332
  (541 shorter events, 112.5 us)
Async XLA Ops:
  7.2 6.9 copy-start
  7.2 74.5 %all-gather.14.cloned.1.call-start = ((), (), s32[]{:S(2)}) async-start(), calls=%async_computation.7 | async-start | bytes 3342336 | tf_op jit(solution)/shard_map/all_gather | solution.py:224
  7.9 88.8 %all-gather.16.cloned.1.call-start = ((), (), s32[]{:S(2)}) async-start(), calls=%async_computation.12 | async-start | bytes 2359296 | tf_op jit(solution)/shard_map/all_gather | solution.py:24
  24.6 7.6 copy-start.84
  24.6 19.6 %copy-start.151 = (f32[768]{0:T(1024)}, f32[768]{0:T(1024)S(1)}, u32[]{:S(2)}) copy-start(f32[768]{0:T(1024)S(1)} %get-tuple-element.76) | copy-start | bytes 9220
  32.2 12.0 slice-start.8
  32.9 11.3 copy-start.34
  32.9 11.3 copy-start.116
  33.1 11.0 copy-start.148
  33.2 11.0 slice-start.9
  45.7 3.8 collective-permute-start
  88.3 58.0 %all-gather.18.cloned.1.call-start = ((), (), s32[]{:S(2)}) async-start(), calls=%async_computation.13 | async-start | bytes 2359296 | tf_op jit(solution)/shard_map/all_gather | solution.py:24
  112.8 12.1 slice-start.10
  113.4 11.4 copy-start.30
  113.4 11.4 copy-start.96
  113.7 11.1 copy-start.119
  113.7 11.1 copy-start.152
  113.7 11.1 slice-start.11
  124.8 5.8 copy-start.29
  127.2 3.4 collective-permute-start.1
  135.0 289.8 %reduce-scatter.26.cloned.1.call-start = ((), (), s32[]{:S(2)}) async-start(), calls=%async_computation.16 | async-start | bytes 417792
  135.1 5.5 copy-start.143
  155.9 6.2 slice-start.4
  159.3 12.5 slice-start.12
  161.8 15.0 %copy-start.33 = (f32[256,768]{1,0:T(8,128)}, f32[256,768]{1,0:T(8,128)S(1)}, u32[]{:S(2)}) copy-start(f32[256,768]{1,0:T(8,128)S(1)} %get-tuple-element.148) | copy-start | bytes 2359300
  161.8 15.0 %copy-start.102 = (f32[256]{0:T(256)}, f32[256]{0:T(256)S(1)}, u32[]{:S(2)}) copy-start(f32[256]{0:T(256)S(1)} %broadcast_multiply_fusion.14) | copy-start | bytes 3076
  162.2 14.6 %copy-start.125 = (f32[256]{0:T(256)}, f32[256]{0:T(256)S(1)}, u32[]{:S(2)}) copy-start(f32[256]{0:T(256)S(1)} %add_rsqrt_fusion) | copy-start | bytes 3076
  162.2 9.5 copy-start.38
  162.2 9.5 slice-start.13
  191.2 3.6 collective-permute-start.2
  202.2 3.8 collective-permute-start.3
  208.1 12.4 copy-start.42
  208.1 7.2 copy-start.31
  208.1 7.2 copy-start.97
  208.1 7.2 copy-start.120
  234.9 3.6 collective-permute-start.4
  245.9 5.6 copy-start.110
  245.9 6.2 copy-start.157
  245.9 6.8 copy-start.155
  245.9 7.4 copy-start.156
  245.9 8.0 copy-start.154
  245.9 8.5 copy-start.113
  246.0 9.1 copy-start.112
  246.0 9.7 copy-start.162
  246.0 10.3 copy-start.159
  246.0 10.9 copy-start.160
  246.0 11.5 copy-start.158
  246.0 12.1 copy-start.25
  246.0 12.1 copy-start.66
  246.0 13.9 %copy-start.58 = (f32[256,768]{1,0:T(8,128)S(1)}, f32[256,768]{1,0:T(8,128)}, u32[]{:S(2)}) copy-start(f32[256,768]{1,0:T(8,128)} %get-tuple-element.161) | copy-start | bytes 2359300
  246.0 13.9 %collective-permute-start.5 = (bf16[256,768]{1,0:T(8,128)(2,1)}, bf16[256,768]{1,0:T(8,128)(2,1)S(1)}, u32[]{:S(2)}, u32[]{:S(2)}) collective-permute-start(bf16[256,768]{1,0:T(8,128)(2,1)} %get-tuple-element.160), channel_id=1, source_target_pairs={{1,0},{3,2},{5,4},{7,6},{9,8},{11,10},{13,12},{15,14},{17,16},{19,... | collective-permute-start | bytes 1179656 | tf_op jit(solution)/shard_map/ppermute | solution.py:20
  247.6 12.4 copy-start.169
  250.9 9.1 copy-start.168
  258.1 7.5 slice-start.6
  260.0 5.5 copy-start.74
  260.1 5.5 copy-start.35
  283.5 249.7 %reduce-scatter.24.cloned.1.call-start = ((), (), s32[]{:S(2)}) async-start(), calls=%async_computation.15 | async-start | bytes 417792
  294.1 364.3 %reduce-scatter.22.cloned.1.call-start = ((), (), s32[]{:S(2)}) async-start(), calls=%async_computation.14 | async-start | bytes 417792
  297.2 494.2 %reduce-scatter.16.cloned.1.call-start = ((), (), s32[]{:S(2)}) async-start(), calls=%async_computation.9 | async-start | bytes 2506752 | tf_op jit(solution)/shard_map/reduce_scatter | solution.py:331
  301.9 645.0 %reduce-scatter.14.cloned.1.call-start = ((), (), s32[]{:S(2)}) async-start(), calls=%async_computation.8 | async-start | bytes 7520256 | tf_op jit(solution)/shard_map/reduce_scatter | solution.py:330
  311.0 811.9 %reduce-scatter.20.cloned.1.call-start = ((), (), s32[]{:S(2)}) async-start(), calls=%async_computation.11 | async-start | bytes 10027008 | tf_op jit(solution)/shard_map/reduce_scatter | solution.py:333
  321.0 978.9 %reduce-scatter.18.cloned.1.call-start = ((), (), s32[]{:S(2)}) async-start(), calls=%async_computation.10 | async-start | bytes 10027008 | tf_op jit(solution)/shard_map/reduce_scatter | solution.py:332
  335.8 85.8 %copy-start.107 = (f32[256]{0:T(256)S(1)}, f32[256]{0:T(256)}, u32[]{:S(2)}) copy-start(f32[256]{0:T(256)} %copy-done.105) | copy-start | bytes 3076
  335.8 85.8 %copy-start.147 = (f32[256]{0:T(256)S(1)}, f32[256]{0:T(256)}, u32[]{:S(2)}) copy-start(f32[256]{0:T(256)} %copy-done.145) | copy-start | bytes 3076
  (136 other events, 357.4 us)
Sparse Core Ops, SparseCore 0:
  10.8 70.8 all-gather.13
  88.4 8.2 all-gather.15
  135.2 11.1 all-gather.17
  283.6 123.6 reduce-scatter.25
  412.5 120.6 reduce-scatter.23
  537.7 120.6 reduce-scatter.21
  664.7 126.6 reduce-scatter.15
  797.3 149.5 reduce-scatter.13
  953.1 169.7 reduce-scatter.19
  1130.0 169.8 reduce-scatter.17
where the time goes:
time: 1320 us; the launch traced here: 1310 us
  waiting for transfers between devices  915 us (69%)
  matrix products  181 us (14%)
  blocking collectives  85 us (6%)
  local copies, waits for them, and re-layouts  48.6 us (4%)
  other arithmetic  47.6 us (4%)
  between operations  17.5 us (1%)
    unnamed x13, waiting for transfers between devices  232 us
    reduce_scatter x1, waiting for transfers between devices, per_device(): lax.psum_scatter(sum_up, 'dp', scatter_dimension=0, tiled=True)  177 us
    reduce_scatter x1, waiting for transfers between devices, per_device(): lax.psum_scatter(sum_down, 'dp', scatter_dimension=0, tiled=True)  176 us
    reduce_scatter x1, waiting for transfers between devices, per_device(): lax.psum_scatter(sum_qkv, 'dp', scatter_dimension=0, tiled=True)  155 us
    reduce_scatter x1, waiting for transfers between devices, per_device(): lax.psum_scatter(sum_out, 'dp', scatter_dimension=0, tiled=True)  132 us
    unnamed x1, blocking collectives  77 us
    all_gather x1, waiting for transfers between devices, fold_backward(): lax.all_gather(codebook, 'dp', axis=0, tiled=True)  32.1 us
    dot_general x3, matrix products, block_forward(): jnp.dot(normed_two_low, w_up, preferred_element_type=jnp.float32) + bias_up  31.6 us
  transfers between devices with their start and end apart: 16, of which 14 were waited for; matrix products, arithmetic and copies ran while one was open for 9% of the time, Pallas kernels for 0%

commit v1 on v0

v1 whole, which is shorter than its diff:
```python
from functools import partial

import jax
import jax.numpy as jnp
from jax import lax
from jax.sharding import PartitionSpec as P

D = 768
HEADS = 12
HD = 64


EPS = 1e-06
MASKED = -1e30


def image_mask(image_lens, row_count):
    limits = jnp.cumsum(image_lens)
    positions = jnp.arange(row_count, dtype=jnp.int32)
    idents = jnp.sum((positions[:, None] >= limits[None, :]).astype(jnp.int32), axis=1)
    return idents[:, None] == idents[None, :]


def norm_parts(values, gains, shifts):
    centre = values - jnp.mean(values, axis=-1, keepdims=True)
    inverse = lax.rsqrt(jnp.mean(centre * centre, axis=-1, keepdims=True) + EPS)
    unit_rows = centre * inverse
    return (unit_rows * gains + shifts, unit_rows, inverse)


def norm_back(grad_rows, unit_rows, inverse, gains):
    scaled = grad_rows * gains
    return inverse * (
        scaled
        - jnp.mean(scaled, axis=-1, keepdims=True)
        - unit_rows * jnp.mean(scaled * unit_rows, axis=-1, keepdims=True)
    )


def head_scores(query_heads, key_heads, same):
    scores = jnp.einsum(
        "bqhd,bkhd->bhqk", query_heads, key_heads, preferred_element_type=jnp.float32
    ) * HD ** (-0.5)
    return jnp.where(same[:, None], scores, MASKED)


def block_forward(inputs, same, weights):
    w_qkv, w_out, w_up, w_down, gains, shifts, bias_out, bias_up = weights
    row_count = inputs.shape[0]
    normed, unit_one, inv_one = norm_parts(inputs, gains[0], shifts[0])
    normed_low = normed.astype(jnp.bfloat16)
    packed = jnp.dot(normed_low, w_qkv, preferred_element_type=jnp.float32).astype(jnp.bfloat16)
    heads = packed.reshape(same.shape[0], -1, 3, HEADS, HD)
    scores = head_scores(heads[:, :, 0], heads[:, :, 1], same)
    highest = jnp.max(scores, axis=-1, keepdims=True)
    powers = jnp.exp(scores - highest)
    totals = jnp.sum(powers, axis=-1, keepdims=True)
    att_probs = powers / totals
    log_total = highest + jnp.log(totals)
    mixed_heads = jnp.einsum(
        "bhqk,bkhd->bqhd",
        att_probs.astype(jnp.bfloat16),
        heads[:, :, 2],
        preferred_element_type=jnp.float32,
    )
    mixed_heads = mixed_heads.reshape(row_count, HEADS * HD).astype(jnp.bfloat16)
    residual = (
        inputs + jnp.dot(mixed_heads, w_out, preferred_element_type=jnp.float32) + bias_out[0]
    )
    normed_two, unit_two, inv_two = norm_parts(residual, gains[1], shifts[1])
    normed_two_low = normed_two.astype(jnp.bfloat16)
    pre_act = jnp.dot(normed_two_low, w_up, preferred_element_type=jnp.float32) + bias_up
    active = jax.nn.gelu(pre_act, approximate=False).astype(jnp.bfloat16)
    output = residual + jnp.dot(active, w_down, preferred_element_type=jnp.float32) + bias_out[1]
    kept_state = (
        unit_one,
        inv_one,
        normed_low,
        packed,
        log_total,
        mixed_heads,
        unit_two,
        inv_two,
        normed_two_low,
        pre_act,
        active,
    )
    return (output, kept_state)


def block_backward(grad_rows, kept_state, same, weights):
    w_qkv, w_out, w_up, w_down, gains, shifts, bias_out, bias_up = weights
    (
        unit_one,
        inv_one,
        normed_low,
        packed,
        log_total,
        mixed_heads,
        unit_two,
        inv_two,
        normed_two_low,
        pre_act,
        active,
    ) = kept_state
    row_count = grad_rows.shape[0]
    grad_low = grad_rows.astype(jnp.bfloat16)
    grad_down = jnp.einsum("rf,rd->fd", active, grad_low, preferred_element_type=jnp.float32)
    d_active = jnp.einsum("rd,fd->rf", grad_low, w_down, preferred_element_type=jnp.float32)
    _, gelu_pull = jax.vjp(partial(jax.nn.gelu, approximate=False), pre_act)
    d_pre = gelu_pull(d_active)[0].astype(jnp.bfloat16)
    grad_up = jnp.einsum("rd,rf->df", normed_two_low, d_pre, preferred_element_type=jnp.float32)
    grad_bias_up = jnp.sum(d_pre.astype(jnp.float32), axis=0)
    d_normed_two = jnp.einsum("rf,df->rd", d_pre, w_up, preferred_element_type=jnp.float32)
    gain_two = jnp.sum(d_normed_two * unit_two, axis=0)
    shift_two = jnp.sum(d_normed_two, axis=0)
    grad_resid = grad_rows + norm_back(d_normed_two, unit_two, inv_two, gains[1])
    resid_low = grad_resid.astype(jnp.bfloat16)
    grad_outw = jnp.einsum("re,rd->ed", mixed_heads, resid_low, preferred_element_type=jnp.float32)
    d_mixed = jnp.einsum("rd,ed->re", resid_low, w_out, preferred_element_type=jnp.float32)
    d_mixed = d_mixed.astype(jnp.bfloat16).reshape(same.shape[0], -1, HEADS, HD)
    heads = packed.reshape(same.shape[0], -1, 3, HEADS, HD)
    query_heads = heads[:, :, 0]
    key_heads = heads[:, :, 1]
    value_heads = heads[:, :, 2]
    att_probs = jnp.exp(head_scores(query_heads, key_heads, same) - log_total)
    d_probs = jnp.einsum("bqhd,bkhd->bhqk", d_mixed, value_heads, preferred_element_type=jnp.float32)
    d_value = jnp.einsum(
        "bhqk,bqhd->bkhd", att_probs.astype(jnp.bfloat16), d_mixed, preferred_element_type=jnp.float32
    )
    d_scores = att_probs * (d_probs - jnp.sum(d_probs * att_probs, axis=-1, keepdims=True))
    d_scores = d_scores.astype(jnp.bfloat16)
    d_query = jnp.einsum(
        "bhqk,bkhd->bqhd", d_scores, key_heads, preferred_element_type=jnp.float32
    ) * HD ** (-0.5)
    d_key = jnp.einsum(
        "bhqk,bqhd->bkhd", d_scores, query_heads, preferred_element_type=jnp.float32
    ) * HD ** (-0.5)
    d_packed = jnp.stack((d_query, d_key, d_value), axis=2).reshape(row_count, 3 * HEADS * HD)
    d_packed = d_packed.astype(jnp.bfloat16)
    grad_qkvw = jnp.einsum("rd,re->de", normed_low, d_packed, preferred_element_type=jnp.float32)
    d_normed = jnp.einsum("re,de->rd", d_packed, w_qkv, preferred_element_type=jnp.float32)
    gain_one = jnp.sum(d_normed * unit_one, axis=0)
    shift_one = jnp.sum(d_normed, axis=0)
    grad_input = grad_resid + norm_back(d_normed, unit_one, inv_one, gains[0])
    grad_parts = (
        grad_qkvw,
        grad_outw,
        grad_up,
        grad_down,
        jnp.stack((gain_one, gain_two)),
        jnp.stack((shift_one, shift_two)),
        jnp.stack((jnp.sum(grad_resid, axis=0), jnp.sum(grad_rows, axis=0))),
        grad_bias_up,
    )
    return (grad_input, grad_parts)


def merge_soft(left_part, right_part):
    highest = jnp.maximum(left_part[0], right_part[0])
    left_factor = jnp.exp(left_part[0] - highest)
    right_factor = jnp.exp(right_part[0] - highest)
    return (
        highest,
        left_part[1] * left_factor + right_part[1] * right_factor,
        left_part[2] * left_factor + right_part[2] * right_factor,
    )


def swapped(value):
    return lax.ppermute(value, "section", [(0, 1), (1, 0)])


def bit_count(size):
    count = size.bit_length() - 1
    return count if size == 1 << count else None


def pick(value, which, axis):
    return lax.dynamic_index_in_dim(value, which, axis, keepdims=False)


def total(terms):
    summed = terms[0].astype(jnp.float32)
    for term in terms[1:]:
        summed = summed + term.astype(jnp.float32)
    return summed


def scatter_sum(rows, order, section):
    size = lax.axis_size("dp")
    count = bit_count(size)
    me = lax.axis_index("dp")
    live = list(range(count))[::-1]
    terms = [rows.reshape((2,) * count + (rows.shape[0] // size,) + rows.shape[1:])]
    for bit in order:
        axis = live.index(bit)
        mine = (me >> bit) & 1
        sent = total([pick(term, 1 - mine, axis) for term in terms]).astype(jnp.bfloat16)
        route = [(2 * i + section, 2 * (i ^ (1 << bit)) + section) for i in range(size)]
        got = lax.ppermute(sent, ("dp", "section"), route)
        terms = [pick(term, mine, axis) for term in terms] + [got]
        live.remove(bit)
    return total(terms)


def gathered(rows):
    size = lax.axis_size("dp")
    count = bit_count(size)
    far = list(range(2, count))
    near = list(range(min(count, 2)))
    half = rows.shape[0] // 2
    out = []
    for piece, order in ((rows[:half], far + near), (rows[half:], far + near[::-1])):
        for bit in order:
            got = lax.ppermute(piece, "dp", [(i, i ^ (1 << bit)) for i in range(size)])
            piece = jnp.concatenate([piece, got])
        out.append(piece)
    return jnp.concatenate(out)


def per_device(
    patches,
    recon_cot,
    lengths,
    codebook,
    w_qkv,
    w_out,
    w_up,
    w_down,
    norm_gain,
    norm_bias,
    bias_out,
    bias_up,
):
    on_first = lax.axis_index("section") == 0
    micro_count = lengths.shape[0]
    row_count = patches.shape[0] // micro_count
    score_scale = D ** (-0.5)
    weights = (
        w_qkv[0],
        w_out[0],
        w_up[0],
        w_down[0],
        norm_gain[0],
        norm_bias[0],
        bias_out[0],
        bias_up[0],
    )
    table = gathered(codebook)
    masks = jax.vmap(partial(image_mask, row_count=row_count))(lengths)
    output, enc_state = block_forward(patches.astype(jnp.float32), masks, weights)
    sent_rows = output.astype(jnp.bfloat16)
    received = lax.ppermute(sent_rows, "section", [(0, 1)])
    hidden_low = jnp.where(on_first, sent_rows, received)
    scores = (
        jnp.einsum("rd,vd->rv", hidden_low, table, preferred_element_type=jnp.float32) * score_scale
    )
    highest = jnp.max(scores, axis=-1, keepdims=True)
    powers = jnp.exp(scores - highest)
    totals = jnp.sum(powers, axis=-1, keepdims=True)
    high_part = powers.astype(jnp.bfloat16)
    low_part = (powers - high_part.astype(jnp.float32)).astype(jnp.bfloat16)
    summed = jnp.dot(high_part, table, preferred_element_type=jnp.float32) + jnp.dot(
        low_part, table, preferred_element_type=jnp.float32
    )
    parts = (highest, totals, summed)
    parts = merge_soft(parts, jax.tree.map(swapped, parts))
    highest, totals, summed = parts
    log_total = highest + jnp.log(totals)
    mean_code = summed / totals
    inverse = lax.rsqrt(jnp.mean(mean_code * mean_code, axis=-1, keepdims=True) + EPS)
    unit_code = mean_code * inverse
    recon, dec_state = block_forward(unit_code, masks, weights)
    grad_unit, dec_parts = block_backward(recon_cot.astype(jnp.float32), dec_state, masks, weights)
    orders = orders_of_bits()
    dec_sums = [
        scatter_sum(part.astype(jnp.bfloat16), order, 1) for part, order in zip(dec_parts[:4], orders)
    ]
    grad_code = inverse * (
        grad_unit - unit_code * jnp.mean(grad_unit * unit_code, axis=-1, keepdims=True)
    )
    own_low = grad_code.astype(jnp.bfloat16)
    got_low = lax.ppermute(own_low, "section", [(1, 0)])
    code_grad_low = jnp.where(on_first, got_low, own_low)
    inner_prod = jnp.sum(code_grad_low.astype(jnp.float32) * mean_code, axis=-1, keepdims=True)
    code_probs = jnp.exp(scores - log_total)
    d_probs = jnp.einsum("rd,vd->rv", code_grad_low, table, preferred_element_type=jnp.float32)
    d_scores = (code_probs * (d_probs - inner_prod)).astype(jnp.bfloat16)
    half_grad = jnp.dot(d_scores, table, preferred_element_type=jnp.float32) * score_scale
    other_half = lax.ppermute(half_grad, "section", [(1, 0)])
    grad_patches, enc_parts = block_backward(half_grad + other_half, enc_state, masks, weights)
    enc_sums = [
        scatter_sum(part.astype(jnp.bfloat16), order, 0) for part, order in zip(enc_parts[:4], orders)
    ]
    size = lax.axis_size("dp")
    small = [jnp.where(on_first, enc, dec) for enc, dec in zip(enc_parts[4:], dec_parts[4:])]
    rows = [part.reshape(2, size, -1).swapaxes(0, 1).reshape(size, -1) for part in small[:3]]
    rows = jnp.concatenate(rows + [small[3].reshape(size, -1)], axis=1)
    share = lax.psum_scatter(rows, "dp", scatter_dimension=0, tiled=True)[0]
    width = D // size
    sums = [jnp.where(on_first, enc, dec)[None] for enc, dec in zip(enc_sums, dec_sums)]
    small_sums = [share[2 * width * i : 2 * width * (i + 1)].reshape(1, 2, width) for i in range(3)]
    ends = jnp.where(on_first, grad_patches, recon)[None]
    return (ends, log_total[:, 0], *sums, *small_sums, share[None, 6 * width :])


def orders_of_bits():
    bits = list(range(bit_count(lax.axis_size("dp"))))
    other = bits[:2][::-1] + bits[2:]
    return [bits, other, other, bits]


def solution(mesh):
    placed = (
        P("dp", None),
        P("dp", None),
        P("dp", None),
        P(("dp", "section"), None),
        P("section", None, None),
        P("section", None, None),
        P("section", None, None),
        P("section", None, None),
        P("section", None, None),
        P("section", None, None),
        P("section", None, None),
        P("section", None),
    )
    return jax.shard_map(
        per_device,
        mesh=mesh,
        in_specs=placed,
        out_specs=(
            P("section", "dp", None),
            P("dp"),
            P("section", "dp", None),
            P("section", "dp", None),
            P("section", "dp", None),
            P("section", "dp", None),
            P("section", None, "dp"),
            P("section", None, "dp"),
            P("section", None, "dp"),
            P("section", "dp"),
        ),
        check_vma=False,
    )
```

time: 1320 us -> 613 us (0.46)
  waiting for transfers between devices: 915 us -> 52.8 us
  starting transfers between devices: 12 us -> 79.5 us
  local copies, waits for them, and re-layouts: 48.6 us -> 116 us
  other arithmetic: 47.6 us -> 94.8 us
  matrix products: 181 us -> 165 us
  between operations: 17.5 us -> 2.89 us
    reduce_scatter x4 -> x0, waiting for transfers between devices: 640 us -> none  [the longest x1 177 us: per_device(): lax.psum_scatter(sum_up, 'dp', scatter_dimension=0, tiled=True)]
    unnamed x13 -> x0, waiting for transfers between devices: 232 us -> none
    ppermute x6 -> x46, starting transfers between devices: 11.1 us -> 79.5 us  [the longest x32 63.2 us: scatter_sum(): got = lax.ppermute(sent, ('dp', 'section'), route)]
    ppermute x6 -> x46, waiting for transfers between devices: 6.76 us -> 52.8 us  [the longest x32 31.2 us: scatter_sum(): got = lax.ppermute(sent, ('dp', 'section'), route)]
    all_gather x3 -> x0, waiting for transfers between devices: 36.9 us -> none  [the longest x1 32.1 us: fold_backward(): lax.all_gather(codebook, 'dp', axis=0, tiled=True)]
    convert_element_type x4 -> x24, other arithmetic: 5.63 us -> 33.6 us  [scatter_sum(): total([pick(term, 1 - mine, axis) for term in terms]).astype(jnp.bfloat16)]
    reshape x0 -> x10, local copies, waits for them, and re-layouts: none -> 24.1 us  [the longest x2 12.1 us: block_forward(): heads = packed.reshape(same.shape[0], -1, 3, HEADS, HD)]
    unnamed x1, blocking collectives: 77 us -> 90.6 us
  transfers between devices with their start and end apart: 16 -> 46, of which waited for: 14 -> 9; matrix products, arithmetic and copies ran while one was open for 9% -> 41% of each run, Pallas kernels for 0% -> 0%
where the time goes in v1:
time: 613 us; the launch traced here: 601 us
  matrix products  165 us (27%)
  local copies, waits for them, and re-layouts  116 us (19%)
  other arithmetic  94.8 us (15%)
  blocking collectives  90.6 us (15%)
  starting transfers between devices  79.5 us (13%)
  waiting for transfers between devices  52.8 us (9%)
    unnamed x1, blocking collectives  90.6 us
    ppermute x32, starting transfers between devices, scatter_sum(): got = lax.ppermute(sent, ('dp', 'section'), route)  63.2 us
    dot_general x2, matrix products, block_forward(): jnp.dot(normed_two_low, w_up, preferred_element_type=jnp.float32) + bias_up  39.6 us
    convert_element_type x24, other arithmetic, scatter_sum(): total([pick(term, 1 - mine, axis) for term in terms]).astype(jnp.bfloat16)  33.6 us
    ppermute x32, waiting for transfers between devices, scatter_sum(): got = lax.ppermute(sent, ('dp', 'section'), route)  31.2 us
    unnamed x265, local copies, waits for them, and re-layouts  29.7 us
    ppermute x8, waiting for transfers between devices, gathered(): got = lax.ppermute(piece, 'dp', [(i, i ^ 1 << bit) for i in range(size)])  21.6 us
    dot_general x2, matrix products, block_backward(): jnp.einsum('rd,fd->rf', grad_low, w_down, preferred_element_type=jnp.floa...  19.4 us
  transfers between devices with their start and end apart: 46, of which 9 were waited for; matrix products, arithmetic and copies ran while one was open for 41% of the time, Pallas kernels for 0%

profile of v1, /device:TPU:0, one launch (start us, length us, event | category | flops | bytes accessed | tf_op | source)
XLA Modules:
  0.0 601.3 jit_solution(2297355095046953047)
XLA Ops:
  2.5 3.0 collective-permute-start.1
  9.8 4.7 convolution_convert_fusion.7
  14.5 4.3 copy.164
  18.8 6.1 %reshape.674 = bf16[2,256,3,12,64]{1,0,4,3,2:T(2,128)(2,1)} reshape(bf16[512,2304]{0,1:T(8,128)(2,1)} %copy.164) | data formatting | bytes 4718592 | tf_op jit(solution)/shard_map/reshape | solution.py:53
  24.9 4.0 fusion.165
  30.0 2.7 fusion.167
  41.1 3.1 collective-permute-start.2
  45.2 12.9 %collective-permute-done.2 = bf16[128,768]{1,0:T(8,128)(2,1)S(1)} collective-permute-done((bf16[128,768]{1,0:T(8,128)(2,1)S(1)}, bf16[128,768]{1,0:T(8,128)(2,1)S(1)}, u32[]{:S(2)}, u32[]{:S(2)}) %collective-permute-start.2) | collective-permute-done | bytes 196640 | tf_op jit(solution)/shard_map/ppermute | solution.py:216
  60.8 18.5 %multiply_convert_fusion.3 = (bf16[512,3072]{1,0:T(8,128)(2,1)S(1)}, f32[512,3072]{1,0:T(8,128)}, f32[512,3072]{1,0:T(8,128)}) fusion(f32[3072]{0:T(1024)S(1)} %bitcast.672, bf16[1,768,3072]{2,1,0:T(8,128)(2,1)S(1)} %bitcast.661, f32[512,768]{1,0:T(8,128)S(1)} %get-tuple-element.65, f32[768]{0:T(1024)S(1)} %get-tuple-element.35, ...), kind=kOutput, calls=%fused_computation.30 | convolution fusion | flops 2521694208 | bytes 22042624 | tf_op jit(solution)/shard_map/dot_general | solution.py:72
  85.4 3.5 add_convert_fusion.4
  88.9 2.5 collective-permute-start
  98.3 8.7 %collective-permute-done.4 = bf16[512,768]{1,0:T(8,128)(2,1)} collective-permute-done((bf16[512,768]{1,0:T(8,128)(2,1)}, bf16[512,768]{1,0:T(8,128)(2,1)}, u32[]{:S(2)}, u32[]{:S(2)}) %collective-permute-start.4) | collective-permute-done | bytes 786464 | tf_op jit(solution)/shard_map/ppermute | solution.py:216
  114.7 4.2 multiply_reduce_fusion.2
  120.9 3.1 fusion.88
  125.4 3.0 fusion.51
  131.7 2.4 multiply_reduce_fusion.13
  135.8 3.7 convolution_convert_fusion.6
  139.4 4.5 copy.170
  143.9 6.0 %reshape.675 = bf16[2,256,3,12,64]{1,0,4,3,2:T(2,128)(2,1)} reshape(bf16[512,2304]{0,1:T(8,128)(2,1)} %copy.170) | data formatting | bytes 4718592 | tf_op jit(solution)/shard_map/reshape | solution.py:53
  149.9 2.9 fusion.164
  161.8 21.0 %multiply_convert_fusion = (bf16[512,3072]{1,0:T(8,128)(2,1)}, f32[512,3072]{1,0:T(8,128)}, f32[512,3072]{1,0:T(8,128)}) fusion(f32[3072]{0:T(1024)S(1)} %bitcast.673, bf16[1,768,3072]{2,1,0:T(8,128)(2,1)S(1)} %bitcast.663, f32[512,768]{1,0:T(8,128)S(1)} %get-tuple-element.72, f32[512]{0:T(512)S(1)} %add_rsqrt_fusion, f32[512]{0:T(512)S(1)} %broadcast_multiply_fusion.9, ...), kind=kOutput, calls=%fused_computation.6 | convolution fusion | flops 2521694208 | bytes 22042624 | tf_op jit(solution)/shard_map/dot_general | solution.py:72
  182.8 9.7 %convert_reduce_fusion = (f32[3072]{0:T(1024)}, bf16[512,3072]{1,0:T(8,128)(2,1)}) fusion(f32[512,3072]{1,0:T(8,128)} %get-tuple-element.42, bf16[512,768]{1,0:T(8,128)(2,1)S(1)} %copy-done.50, bf16[1,3072,768]{2,1,0:T(8,128)(2,1)S(1)} %bitcast.669, f32[512,3072]{1,0:T(8,128)} %get-tuple-element.73, f32[3072]{0:T(1024)S(1)} %bitcast.674), kind=kOutput, calls=%fused_computation.4 | convolution fusion | flops 2442654720 | bytes 21258240 | tf_op jit(solution)/shard_map/rd,fd->rf/dot_general | solution.py:109
  192.6 5.6 multiply_reduce_fusion.3
  204.7 3.3 reshape.676
  208.1 7.5 %multiply_reduce_fusion.1 = (f32[2,12,256]{2,1,0:T(8,128)S(1)}, f32[2,12,256,256]{2,3,1,0:T(8,128)}) fusion(f32[2,12,256,256]{2,3,1,0:T(8,128)} %copy-done.2, f32[2,12,256]{2,1,0:T(8,128)} %log_add_fusion.1, bf16[2,256,1,12,64]{1,0,4,3,2:T(2,128)(2,1)} %copy-done.36, bf16[2,256,12,64]{1,0,3,2:T(2,128)(2,1)} %reshape.676), kind=kOutput, calls=%fused_computation.12 | convolution fusion | flops 206039040 | bytes 14204928 | tf_op jit(solution)/shard_map/bqhd,bkhd->bhqk/dot_general | solution.py:127
  215.6 6.3 %multiply_convert_fusion.2 = bf16[2,12,256,256]{2,3,1,0:T(8,128)(2,1)S(1)} fusion(f32[2,12,256,256]{2,3,1,0:T(8,128)} %get-tuple-element.76, f32[2,12,256,256]{2,3,1,0:T(8,128)} %copy-done.2, f32[2,12,256]{2,1,0:T(8,128)S(1)} %get-tuple-element.75, f32[2,12,256]{2,1,0:T(8,128)S(1)} %copy-done.53), kind=kLoop, calls=%fused_computation.11 | loop fusion | flops 6291456 | bytes 15777792 | tf_op jit(solution)/shard_map/convert_element_type | solution.py:132
  226.9 2.5 copy.182
  230.8 2.5 multiply_reduce_fusion.17
  233.3 2.6 convolution_convert_fusion.4
  244.3 4.8 convolution_convert_fusion.2
  252.2 9.0 %convolution_multiply_fusion = f32[512,768]{1,0:T(8,128)} fusion(bf16[2048,768]{1,0:T(8,128)(2,1)} %constant_dynamic-update-slice_fusion, f32[512,2048]{1,0:T(8,128)} %copy-done.25, f32[512]{0:T(512)S(1)} %multiply_reduce_fusion.7, f32[512]{0:T(512)S(1)} %bitcast.659, bf16[512,768]{1,0:T(8,128)(2,1)} %copy-done.49, bf16[512,768]{1,0:T(8,128)(2,1)} %copy-done.43, ...), kind=kOutput, calls=%fused_computation.171 | convolution fusion | flops 3227254784 | bytes 10489857 | tf_op jit(solution)/shard_map/dot_general | solution.py:290
  262.6 6.9 %convolution_convert_fusion = bf16[3072,768]{1,0:T(8,128)(2,1)} fusion(bf16[512,3072]{1,0:T(8,128)(2,1)} %get-tuple-element.41, bf16[512,768]{1,0:T(8,128)(2,1)} %param.13), kind=kOutput, calls=%fused_computation.50 | convolution fusion | flops 2418278400 | bytes 8650752 | tf_op jit(solution)/shard_map/rf,rd->fd/dot_general | solution.py:108
  276.2 3.2 dynamic-slice_bitcast_fusion
  283.6 3.3 dynamic-slice_bitcast_fusion.2
  290.6 2.8 fusion.69
  297.4 9.7 %convert_reduce_fusion.1 = (f32[3072]{0:T(1024)}, bf16[512,3072]{1,0:T(8,128)(2,1)S(1)}) fusion(f32[512,3072]{1,0:T(8,128)} %get-tuple-element.50, bf16[1,3072,768]{2,1,0:T(8,128)(2,1)} %param.19, f32[512,768]{1,0:T(8,128)S(1)} %get-tuple-element.40, f32[512,3072]{1,0:T(8,128)} %get-tuple-element.66, f32[3072]{0:T(1024)S(1)} %bitcast.675), kind=kOutput, calls=%fused_computation.5 | convolution fusion | flops 2443047936 | bytes 22044672 | tf_op jit(solution)/shard_map/rd,fd->rf/dot_general | solution.py:109
  307.2 3.6 multiply_reduce_fusion.5
  317.1 3.3 reshape.677
  320.5 7.5 %multiply_reduce_fusion = (f32[2,12,256]{2,1,0:T(8,128)S(1)}, f32[2,12,256,256]{2,3,1,0:T(8,128)}) fusion(f32[2,12,256,256]{2,3,1,0:T(8,128)} %copy-done.1, f32[2,12,256]{2,1,0:T(8,128)} %log_add_fusion, bf16[2,256,1,12,64]{1,0,4,3,2:T(2,128)(2,1)} %get-tuple-element.54, bf16[2,256,12,64]{1,0,3,2:T(2,128)(2,1)} %reshape.677), kind=kOutput, calls=%fused_computation.8 | convolution fusion | flops 206039040 | bytes 14204928 | tf_op jit(solution)/shard_map/bqhd,bkhd->bhqk/dot_general | solution.py:127
  328.0 6.3 %multiply_convert_fusion.1 = bf16[2,12,256,256]{2,3,1,0:T(8,128)(2,1)S(1)} fusion(f32[2,12,256,256]{2,3,1,0:T(8,128)} %get-tuple-element.80, f32[2,12,256,256]{2,3,1,0:T(8,128)} %copy-done.1, f32[2,12,256]{2,1,0:T(8,128)S(1)} %get-tuple-element.79, f32[2,12,256]{2,1,0:T(8,128)S(1)} %copy-done.52), kind=kLoop, calls=%fused_computation.7 | loop fusion | flops 6291456 | bytes 15777792 | tf_op jit(solution)/shard_map/convert_element_type | solution.py:132
  339.0 2.9 convolution_convert_fusion.1
  342.0 3.6 convolution_convert_fusion.3
  346.7 2.5 copy.189
  350.3 3.1 fusion.79
  355.0 2.5 collective-permute-start.38
  360.0 3.5 collective-permute-start.22
  363.6 2.4 convolution_convert_fusion.5
  367.6 4.1 fusion.78
  383.4 2.5 collective-permute-start.30
  391.5 3.5 collective-permute-start.14
  396.5 90.6 %all-reduce = f32[16,480]{1,0:T(8,128)} all-reduce(f32[16,480]{1,0:T(8,128)} %pad_maximum_fusion.6), channel_id=2, replica_groups=mesh['dp'=16,'section'=2] {'dp'}, use_global_device_ids=true, to_apply=%region_43.44.clone | all-reduce | flops 7680 | bytes 61440
  500.0 8.4 %collective-permute-done.23 = bf16[2,2,48,768]{3,2,1,0:T(8,128)(2,1)S(1)} collective-permute-done((bf16[2,2,48,768]{3,2,1,0:T(8,128)(2,1)S(1)}, bf16[2,2,48,768]{3,2,1,0:T(8,128)(2,1)S(1)}, u32[]{:S(2)}, u32[]{:S(2)}) %collective-permute-start.23) | collective-permute-done | bytes 294944 | tf_op jit(solution)/shard_map/ppermute | solution.py:201
  515.5 3.9 collective-permute-done.24
  531.2 3.9 collective-permute-start.39
  546.6 10.3 %collective-permute-done.39 = bf16[2,2,192,768]{3,2,1,0:T(8,128)(2,1)S(1)} collective-permute-done((bf16[2,2,192,768]{3,2,1,0:T(8,128)(2,1)S(1)}, bf16[2,2,192,768]{3,2,1,0:T(8,128)(2,1)S(1)}, u32[]{:S(2)}, u32[]{:S(2)}) %collective-permute-start.39) | collective-permute-done | bytes 1179680 | tf_op jit(solution)/shard_map/ppermute | solution.py:201
  556.9 3.2 collective-permute-start.16
  561.4 2.6 collective-permute-start.40
  565.4 3.2 collective-permute-start.32
  573.4 4.8 collective-permute-start.17
  579.7 4.8 collective-permute-start.41
  590.0 2.4 collective-permute-done.41
  592.4 2.4 fusion.121
  594.7 4.0 collective-permute-done.33
  598.7 2.4 fusion.127
  (474 shorter events, 195.6 us)
Async XLA Ops:
  2.5 36.9 %collective-permute-start.1 = (bf16[64,768]{1,0:T(8,128)(2,1)}, bf16[64,768]{1,0:T(8,128)(2,1)}, u32[]{:S(2)}, u32[]{:S(2)}) collective-permute-start(bf16[64,768]{1,0:T(8,128)(2,1)} %get-tuple-element.61), channel_id=1, source_target_pairs={{0,8},{2,10},{4,12},{6,14},{8,0},{10,2},{12,4},{14,6},{16,24},{18,... | collective-permute-start | bytes 294920 | tf_op jit(solution)/shard_map/ppermute | solution.py:216
  5.5 38.7 %collective-permute-start.5 = (bf16[64,768]{1,0:T(8,128)(2,1)}, bf16[64,768]{1,0:T(8,128)(2,1)}, u32[]{:S(2)}, u32[]{:S(2)}) collective-permute-start(bf16[64,768]{1,0:T(8,128)(2,1)} %get-tuple-element.59), channel_id=1, source_target_pairs={{0,8},{2,10},{4,12},{6,14},{8,0},{10,2},{12,4},{14,6},{16,24},{18,... | collective-permute-start | bytes 294920 | tf_op jit(solution)/shard_map/ppermute | solution.py:216
  9.2 51.6 %copy-start.83 = (f32[768]{0:T(1024)}, f32[768]{0:T(1024)S(1)}, u32[]{:S(2)}) copy-start(f32[768]{0:T(1024)S(1)} %get-tuple-element.35) | copy-start | bytes 9220
  37.4 23.4 %slice-start.8 = ((s8[4718592]{0:T(1024)(128)(4,1)}), s8[4194304]{0:T(1024)(128)(4,1)S(1)}, s32[]{:S(2)}) async-start(s8[4718592]{0:T(1024)(128)(4,1)} %bitcast.660), calls=%async_computation.8 | async-start | bytes 8388608
  37.7 47.7 %copy-start.81 = (f32[768]{0:T(1024)}, f32[768]{0:T(1024)S(1)}, u32[]{:S(2)}) copy-start(f32[768]{0:T(1024)S(1)} %get-tuple-element.31) | copy-start | bytes 9220
  38.1 22.7 %copy-start.97 = (f32[1,3072]{1,0:T(1,128)S(1)}, f32[1,3072]{1,0:T(1,128)}, u32[]{:S(2)}) copy-start(f32[1,3072]{1,0:T(1,128)} %param.23) | copy-start | bytes 36868
  39.0 46.3 %copy-start.12 = (f32[512,768]{1,0:T(8,128)}, f32[512,768]{1,0:T(8,128)S(1)}, u32[]{:S(2)}) copy-start(f32[512,768]{1,0:T(8,128)S(1)} %get-tuple-element.65) | copy-start | bytes 4718596
  39.1 40.3 %copy-start.62 = (f32[512]{0:T(512)}, f32[512]{0:T(512)S(1)}, u32[]{:S(2)}) copy-start(f32[512]{0:T(512)S(1)} %broadcast_multiply_fusion.11) | copy-start | bytes 6148
  39.1 46.3 %slice-start.14 = ((s8[4718592]{0:T(1024)(128)(4,1)}), s8[4194304]{0:T(1024)(128)(4,1)S(1)}, s32[]{:S(2)}) async-start(s8[4718592]{0:T(1024)(128)(4,1)} %bitcast.666), calls=%async_computation.14 | async-start | bytes 8388608
  41.1 17.0 %collective-permute-start.2 = (bf16[128,768]{1,0:T(8,128)(2,1)S(1)}, bf16[128,768]{1,0:T(8,128)(2,1)S(1)}, u32[]{:S(2)}, u32[]{:S(2)}) collective-permute-start(bf16[128,768]{1,0:T(8,128)(2,1)S(1)} %pad_maximum_fusion.4), channel_id=1, source_target_pairs={{0,16},{2,18},{4,20},{6,22},{8,24},{10,26},{12,28},{14,30},{16,0},... | collective-permute-start | bytes 589832 | tf_op jit(solution)/shard_map/ppermute | solution.py:216
  44.2 35.2 %copy-start.72 = (f32[512]{0:T(512)}, f32[512]{0:T(512)S(1)}, u32[]{:S(2)}) copy-start(f32[512]{0:T(512)S(1)} %add_rsqrt_fusion.3) | copy-start | bytes 6148
  45.1 34.2 %collective-permute-start.6 = (bf16[128,768]{1,0:T(8,128)(2,1)S(1)}, bf16[128,768]{1,0:T(8,128)(2,1)S(1)}, u32[]{:S(2)}, u32[]{:S(2)}) collective-permute-start(bf16[128,768]{1,0:T(8,128)(2,1)S(1)} %pad_maximum_fusion.5), channel_id=1, source_target_pairs={{0,16},{2,18},{4,20},{6,22},{8,24},{10,26},{12,28},{14,30},{16,0},... | collective-permute-start | bytes 589832 | tf_op jit(solution)/shard_map/ppermute | solution.py:216
  58.1 24.7 %copy-start.46 = (bf16[128,768]{1,0:T(8,128)(2,1)}, bf16[128,768]{1,0:T(8,128)(2,1)S(1)}, u32[]{:S(2)}) copy-start(bf16[128,768]{1,0:T(8,128)(2,1)S(1)} %collective-permute-done.2) | copy-start | bytes 589828
  59.2 23.6 %collective-permute-start.3 = (bf16[256,768]{1,0:T(8,128)(2,1)S(1)}, bf16[256,768]{1,0:T(8,128)(2,1)S(1)}, u32[]{:S(2)}, u32[]{:S(2)}) collective-permute-start(bf16[256,768]{1,0:T(8,128)(2,1)S(1)} %pad_maximum_fusion.2), channel_id=1, source_target_pairs={{0,2},{2,0},{4,6},{6,4},{8,10},{10,8},{12,14},{14,12},{16,18},{18,... | collective-permute-start | bytes 1179656 | tf_op jit(solution)/shard_map/ppermute | solution.py:216
  60.8 24.6 %slice-start.15 = ((s8[4718592]{0:T(1024)(128)(4,1)}), s8[524288]{0:T(1024)(128)(4,1)S(1)}, s32[]{:S(2)}) async-start(s8[4718592]{0:T(1024)(128)(4,1)} %bitcast.666), calls=%async_computation.15 | async-start | bytes 1048576
  81.3 13.4 %collective-permute-start.7 = (bf16[256,768]{1,0:T(8,128)(2,1)}, bf16[256,768]{1,0:T(8,128)(2,1)}, u32[]{:S(2)}, u32[]{:S(2)}) collective-permute-start(bf16[256,768]{1,0:T(8,128)(2,1)} %pad_maximum_fusion.3), channel_id=1, source_target_pairs={{0,4},{2,6},{4,0},{6,2},{8,12},{10,14},{12,8},{14,10},{16,20},{18,... | collective-permute-start | bytes 1179656 | tf_op jit(solution)/shard_map/ppermute | solution.py:216
  84.8 22.1 %collective-permute-start.4 = (bf16[512,768]{1,0:T(8,128)(2,1)}, bf16[512,768]{1,0:T(8,128)(2,1)}, u32[]{:S(2)}, u32[]{:S(2)}) collective-permute-start(bf16[512,768]{1,0:T(8,128)(2,1)} %pad_maximum_fusion), channel_id=1, source_target_pairs={{0,4},{2,6},{4,0},{6,2},{8,12},{10,14},{12,8},{14,10},{16,20},{18,... | collective-permute-start | bytes 2359304 | tf_op jit(solution)/shard_map/ppermute | solution.py:216
  88.9 25.8 %collective-permute-start = (bf16[512,768]{1,0:T(8,128)(2,1)}, bf16[512,768]{1,0:T(8,128)(2,1)}, u32[]{:S(2)}, u32[]{:S(2)}) collective-permute-start(bf16[512,768]{1,0:T(8,128)(2,1)} %add_convert_fusion.4), channel_id=1, source_target_pairs={{0,1},{2,3},{4,5},{6,7},{8,9},{10,11},{12,13},{14,15},{16,17},{18,... | collective-permute-start | bytes 2359304 | tf_op jit(solution)/shard_map/ppermute | solution.py:254
  95.9 17.8 %collective-permute-start.8 = (bf16[512,768]{1,0:T(8,128)(2,1)S(1)}, bf16[512,768]{1,0:T(8,128)(2,1)S(1)}, u32[]{:S(2)}, u32[]{:S(2)}) collective-permute-start(bf16[512,768]{1,0:T(8,128)(2,1)S(1)} %pad_maximum_fusion.1), channel_id=1, source_target_pairs={{0,2},{2,0},{4,6},{6,4},{8,10},{10,8},{12,14},{14,12},{16,18},{18,... | collective-permute-start | bytes 2359304 | tf_op jit(solution)/shard_map/ppermute | solution.py:216
  124.0 7.6 %collective-permute-start.11 = (f32[512,768]{1,0:T(8,128)}, f32[512,768]{1,0:T(8,128)}, u32[]{:S(2)}, u32[]{:S(2)}) collective-permute-start(f32[512,768]{1,0:T(8,128)} %fusion.88), channel_id=1, source_target_pairs={{0,1},{1,0},{2,3},{3,2},{4,5},{5,4},{6,7},{7,6},{8,9},{9,8},{10,11... | collective-permute-start | bytes 4718600 | tf_op jit(solution)/shard_map/ppermute | solution.py:171
  128.4 2.0 collective-permute-start.10
  129.0 1.4 collective-permute-start.9
  161.3 36.9 %copy-start.15 = (f32[512,768]{1,0:T(8,128)}, f32[512,768]{1,0:T(8,128)S(1)}, u32[]{:S(2)}) copy-start(f32[512,768]{1,0:T(8,128)S(1)} %get-tuple-element.72) | copy-start | bytes 4718596
  161.4 36.9 %copy-start.66 = (f32[512]{0:T(512)}, f32[512]{0:T(512)S(1)}, u32[]{:S(2)}) copy-start(f32[512]{0:T(512)S(1)} %broadcast_multiply_fusion.9) | copy-start | bytes 6148
  161.7 36.5 %copy-start.74 = (f32[512]{0:T(512)}, f32[512]{0:T(512)S(1)}, u32[]{:S(2)}) copy-start(f32[512]{0:T(512)S(1)} %add_rsqrt_fusion) | copy-start | bytes 6148
  238.9 12.5 %collective-permute-start.12 = (bf16[512,768]{1,0:T(8,128)(2,1)S(1)}, bf16[512,768]{1,0:T(8,128)(2,1)S(1)}, u32[]{:S(2)}, u32[]{:S(2)}) collective-permute-start(bf16[512,768]{1,0:T(8,128)(2,1)S(1)} %multiply_convert_fusion.5), channel_id=1, source_target_pairs={{1,0},{3,2},{5,4},{7,6},{9,8},{11,10},{13,12},{15,14},{17,16},{19,... | collective-permute-start | bytes 2359304 | tf_op jit(solution)/shard_map/ppermute | solution.py:284
  240.3 8.8 %collective-permute-start.26 = (bf16[2,2,2,48,768]{4,3,2,1,0:T(8,128)(2,1)S(1)}, bf16[2,2,2,48,768]{4,3,2,1,0:T(8,128)(2,1)S(1)}, u32[]{:S(2)}, u32[]{:S(2)}) collective-permute-start(bf16[2,2,2,48,768]{4,3,2,1,0:T(8,128)(2,1)S(1)} %dynamic-slice_bitcast_fusion.6), channel_id=1, source_target_pairs={{1,5},{3,7},{5,1},{7,3},{9,13},{11,15},{13,9},{15,11},{17,21},{19,... | collective-permute-start | bytes 1769480 | tf_op jit(solution)/shard_map/ppermute | solution.py:201
  242.4 48.2 %collective-permute-start.18 = (bf16[2,2,2,48,2304]{4,3,2,1,0:T(8,128)(2,1)}, bf16[2,2,2,48,2304]{4,3,2,1,0:T(8,128)(2,1)}, u32[]{:S(2)}, u32[]{:S(2)}) collective-permute-start(bf16[2,2,2,48,2304]{4,3,2,1,0:T(8,128)(2,1)} %dynamic-slice_bitcast_fusion.4), channel_id=1, source_target_pairs={{1,3},{3,1},{5,7},{7,5},{9,11},{11,9},{13,15},{15,13},{17,19},{19,... | collective-permute-start | bytes 5308424 | tf_op jit(solution)/shard_map/ppermute | solution.py:201
  249.9 31.6 %collective-permute-start.27 = (bf16[2,2,48,768]{3,2,1,0:T(8,128)(2,1)}, bf16[2,2,48,768]{3,2,1,0:T(8,128)(2,1)}, u32[]{:S(2)}, u32[]{:S(2)}) collective-permute-start(bf16[2,2,48,768]{3,2,1,0:T(8,128)(2,1)} %fusion.130), channel_id=1, source_target_pairs={{1,3},{3,1},{5,7},{7,5},{9,11},{11,9},{13,15},{15,13},{17,19},{19,... | collective-permute-start | bytes 884744 | tf_op jit(solution)/shard_map/ppermute | solution.py:201
  261.3 33.8 %collective-permute-start.13 = (f32[512,768]{1,0:T(8,128)}, f32[512,768]{1,0:T(8,128)}, u32[]{:S(2)}, u32[]{:S(2)}) collective-permute-start(f32[512,768]{1,0:T(8,128)} %convolution_multiply_fusion), channel_id=1, source_target_pairs={{1,0},{3,2},{5,4},{7,6},{9,8},{11,10},{13,12},{15,14},{17,16},{19,... | collective-permute-start | bytes 4718600 | tf_op jit(solution)/shard_map/ppermute | solution.py:291
  279.5 103.9 %collective-permute-start.42 = (bf16[2,2,2,192,768]{4,3,2,1,0:T(8,128)(2,1)}, bf16[2,2,2,192,768]{4,3,2,1,0:T(8,128)(2,1)}, u32[]{:S(2)}, u32[]{:S(2)}) collective-permute-start(bf16[2,2,2,192,768]{4,3,2,1,0:T(8,128)(2,1)} %dynamic-slice_bitcast_fusion), channel_id=1, source_target_pairs={{1,3},{3,1},{5,7},{7,5},{9,11},{11,9},{13,15},{15,13},{17,19},{19,... | collective-permute-start | bytes 7077896 | tf_op jit(solution)/shard_map/ppermute | solution.py:201
  282.7 6.3 %collective-permute-start.28 = (bf16[2,48,768]{2,1,0:T(8,128)(2,1)S(1)}, bf16[2,48,768]{2,1,0:T(8,128)(2,1)S(1)}, u32[]{:S(2)}, u32[]{:S(2)}) collective-permute-start(bf16[2,48,768]{2,1,0:T(8,128)(2,1)S(1)} %fusion.144), channel_id=1, source_target_pairs={{1,9},{3,11},{5,13},{7,15},{9,1},{11,3},{13,5},{15,7},{17,25},{19,... | collective-permute-start | bytes 442376 | tf_op jit(solution)/shard_map/ppermute | solution.py:201
  286.9 208.8 %collective-permute-start.34 = (bf16[2,2,2,48,3072]{4,3,2,1,0:T(8,128)(2,1)}, bf16[2,2,2,48,3072]{4,3,2,1,0:T(8,128)(2,1)}, u32[]{:S(2)}, u32[]{:S(2)}) collective-permute-start(bf16[2,2,2,48,3072]{4,3,2,1,0:T(8,128)(2,1)} %dynamic-slice_bitcast_fusion.2), channel_id=1, source_target_pairs={{1,5},{3,7},{5,1},{7,3},{9,13},{11,15},{13,9},{15,11},{17,21},{19,... | collective-permute-start | bytes 7077896 | tf_op jit(solution)/shard_map/ppermute | solution.py:201
  293.4 203.2 %collective-permute-start.19 = (bf16[2,2,48,2304]{3,2,1,0:T(8,128)(2,1)}, bf16[2,2,48,2304]{3,2,1,0:T(8,128)(2,1)}, u32[]{:S(2)}, u32[]{:S(2)}) collective-permute-start(bf16[2,2,48,2304]{3,2,1,0:T(8,128)(2,1)} %fusion.69), channel_id=1, source_target_pairs={{1,5},{3,7},{5,1},{7,3},{9,13},{11,15},{13,9},{15,11},{17,21},{19,... | collective-permute-start | bytes 2654216 | tf_op jit(solution)/shard_map/ppermute | solution.py:201
  355.0 171.8 %collective-permute-start.38 = (bf16[2,2,2,192,768]{4,3,2,1,0:T(8,128)(2,1)}, bf16[2,2,2,192,768]{4,3,2,1,0:T(8,128)(2,1)}, u32[]{:S(2)}, u32[]{:S(2)}) collective-permute-start(bf16[2,2,2,192,768]{4,3,2,1,0:T(8,128)(2,1)} %dynamic-slice_bitcast_fusion.1), channel_id=1, source_target_pairs={{0,2},{2,0},{4,6},{6,4},{8,10},{10,8},{12,14},{14,12},{16,18},{18,... | collective-permute-start | bytes 7077896 | tf_op jit(solution)/shard_map/ppermute | solution.py:201
  360.0 31.5 %collective-permute-start.22 = (bf16[2,2,2,48,768]{4,3,2,1,0:T(8,128)(2,1)}, bf16[2,2,2,48,768]{4,3,2,1,0:T(8,128)(2,1)}, u32[]{:S(2)}, u32[]{:S(2)}) collective-permute-start(bf16[2,2,2,48,768]{4,3,2,1,0:T(8,128)(2,1)} %dynamic-slice_bitcast_fusion.7), channel_id=1, source_target_pairs={{0,4},{2,6},{4,0},{6,2},{8,12},{10,14},{12,8},{14,10},{16,20},{18,... | collective-permute-start | bytes 1769480 | tf_op jit(solution)/shard_map/ppermute | solution.py:201
  383.4 147.8 %collective-permute-start.30 = (bf16[2,2,2,48,3072]{4,3,2,1,0:T(8,128)(2,1)}, bf16[2,2,2,48,3072]{4,3,2,1,0:T(8,128)(2,1)}, u32[]{:S(2)}, u32[]{:S(2)}) collective-permute-start(bf16[2,2,2,48,3072]{4,3,2,1,0:T(8,128)(2,1)} %dynamic-slice_bitcast_fusion.3), channel_id=1, source_target_pairs={{0,4},{2,6},{4,0},{6,2},{8,12},{10,14},{12,8},{14,10},{16,20},{18,... | collective-permute-start | bytes 7077896 | tf_op jit(solution)/shard_map/ppermute | solution.py:201
  391.5 131.9 %collective-permute-start.14 = (bf16[2,2,2,48,2304]{4,3,2,1,0:T(8,128)(2,1)}, bf16[2,2,2,48,2304]{4,3,2,1,0:T(8,128)(2,1)}, u32[]{:S(2)}, u32[]{:S(2)}) collective-permute-start(bf16[2,2,2,48,2304]{4,3,2,1,0:T(8,128)(2,1)} %dynamic-slice_bitcast_fusion.5), channel_id=1, source_target_pairs={{0,2},{2,0},{4,6},{6,4},{8,10},{10,8},{12,14},{14,12},{16,18},{18,... | collective-permute-start | bytes 5308424 | tf_op jit(solution)/shard_map/ppermute | solution.py:201
  492.6 35.1 %slice-start.6 = ((s8[4718592]{0:T(1024)(128)(4,1)}), s8[4194304]{0:T(1024)(128)(4,1)S(1)}, s32[]{:S(2)}) async-start(s8[4718592]{0:T(1024)(128)(4,1)} %bitcast.615), calls=%async_computation.6 | async-start | bytes 8388608
  495.7 23.8 %copy-start.61 = (bf16[48,768]{1,0:T(8,128)(2,1)S(1)}, bf16[48,768]{1,0:T(8,128)(2,1)}, u32[]{:S(2)}) copy-start(bf16[48,768]{1,0:T(8,128)(2,1)} %fusion.146) | copy-start | bytes 221188
  495.7 25.4 %collective-permute-start.43 = (bf16[2,2,192,768]{3,2,1,0:T(8,128)(2,1)S(1)}, bf16[2,2,192,768]{3,2,1,0:T(8,128)(2,1)S(1)}, u32[]{:S(2)}, u32[]{:S(2)}) collective-permute-start(bf16[2,2,192,768]{3,2,1,0:T(8,128)(2,1)S(1)} %fusion.54), channel_id=1, source_target_pairs={{1,5},{3,7},{5,1},{7,3},{9,13},{11,15},{13,9},{15,11},{17,21},{19,... | collective-permute-start | bytes 3538952 | tf_op jit(solution)/shard_map/ppermute | solution.py:201
  496.6 11.8 %collective-permute-start.23 = (bf16[2,2,48,768]{3,2,1,0:T(8,128)(2,1)S(1)}, bf16[2,2,48,768]{3,2,1,0:T(8,128)(2,1)S(1)}, u32[]{:S(2)}, u32[]{:S(2)}) collective-permute-start(bf16[2,2,48,768]{3,2,1,0:T(8,128)(2,1)S(1)} %fusion.131), channel_id=1, source_target_pairs={{0,2},{2,0},{4,6},{6,4},{8,10},{10,8},{12,14},{14,12},{16,18},{18,... | collective-permute-start | bytes 884744 | tf_op jit(solution)/shard_map/ppermute | solution.py:201
  500.0 25.4 %copy-start.28 = (bf16[768,2304]{1,0:T(8,128)(2,1)S(1)}, bf16[768,2304]{1,0:T(8,128)(2,1)}, u32[]{:S(2)}) copy-start(bf16[768,2304]{1,0:T(8,128)(2,1)} %copy-done.27) | copy-start | bytes 10616836
  500.0 27.7 %slice-start.7 = ((s8[4718592]{0:T(1024)(128)(4,1)}), s8[524288]{0:T(1024)(128)(4,1)S(1)}, s32[]{:S(2)}) async-start(s8[4718592]{0:T(1024)(128)(4,1)} %bitcast.615), calls=%async_computation.7 | async-start | bytes 1048576
  508.4 3.9 collective-permute-start.20
  509.1 26.0 %slice-start.4 = ((s8[4718592]{0:T(1024)(128)(4,1)}), s8[4194304]{0:T(1024)(128)(4,1)S(1)}, s32[]{:S(2)}) async-start(s8[4718592]{0:T(1024)(128)(4,1)} %bitcast.608), calls=%async_computation.4 | async-start | bytes 8388608
  512.3 7.1 %collective-permute-start.24 = (bf16[2,48,768]{2,1,0:T(8,128)(2,1)S(1)}, bf16[2,48,768]{2,1,0:T(8,128)(2,1)S(1)}, u32[]{:S(2)}, u32[]{:S(2)}) collective-permute-start(bf16[2,48,768]{2,1,0:T(8,128)(2,1)S(1)} %fusion.145), channel_id=1, source_target_pairs={{0,8},{2,10},{4,12},{6,14},{8,0},{10,2},{12,4},{14,6},{16,24},{18,... | collective-permute-start | bytes 442376 | tf_op jit(solution)/shard_map/ppermute | solution.py:201
  519.5 9.8 %collective-permute-start.29 = (bf16[48,768]{1,0:T(8,128)(2,1)S(1)}, bf16[48,768]{1,0:T(8,128)(2,1)S(1)}, u32[]{:S(2)}, u32[]{:S(2)}) collective-permute-start(bf16[48,768]{1,0:T(8,128)(2,1)S(1)} %copy-done.61), channel_id=1, source_target_pairs={{1,17},{3,19},{5,21},{7,23},{9,25},{11,27},{13,29},{15,31},{17,1},... | collective-permute-start | bytes 221192 | tf_op jit(solution)/shard_map/ppermute | solution.py:201
  521.1 19.5 %collective-permute-start.35 = (bf16[2,2,48,3072]{3,2,1,0:T(8,128)(2,1)S(1)}, bf16[2,2,48,3072]{3,2,1,0:T(8,128)(2,1)S(1)}, u32[]{:S(2)}, u32[]{:S(2)}) collective-permute-start(bf16[2,2,48,3072]{3,2,1,0:T(8,128)(2,1)S(1)} %fusion.56), channel_id=1, source_target_pairs={{1,3},{3,1},{5,7},{7,5},{9,11},{11,9},{13,15},{15,13},{17,19},{19,... | collective-permute-start | bytes 3538952 | tf_op jit(solution)/shard_map/ppermute | solution.py:201
  523.5 13.4 %collective-permute-start.25 = (bf16[48,768]{1,0:T(8,128)(2,1)S(1)}, bf16[48,768]{1,0:T(8,128)(2,1)S(1)}, u32[]{:S(2)}, u32[]{:S(2)}) collective-permute-start(bf16[48,768]{1,0:T(8,128)(2,1)S(1)} %fusion.150), channel_id=1, source_target_pairs={{0,16},{2,18},{4,20},{6,22},{8,24},{10,26},{12,28},{14,30},{16,0},... | collective-permute-start | bytes 221192 | tf_op jit(solution)/shard_map/ppermute | solution.py:201
  526.8 15.9 %collective-permute-start.44 = (bf16[2,192,768]{2,1,0:T(8,128)(2,1)S(1)}, bf16[2,192,768]{2,1,0:T(8,128)(2,1)S(1)}, u32[]{:S(2)}, u32[]{:S(2)}) collective-permute-start(bf16[2,192,768]{2,1,0:T(8,128)(2,1)S(1)} %fusion.99), channel_id=1, source_target_pairs={{1,9},{3,11},{5,13},{7,15},{9,1},{11,3},{13,5},{15,7},{17,25},{19,... | collective-permute-start | bytes 1769480 | tf_op jit(solution)/shard_map/ppermute | solution.py:201
  529.3 15.4 %collective-permute-start.15 = (bf16[2,2,48,2304]{3,2,1,0:T(8,128)(2,1)S(1)}, bf16[2,2,48,2304]{3,2,1,0:T(8,128)(2,1)S(1)}, u32[]{:S(2)}, u32[]{:S(2)}) collective-permute-start(bf16[2,2,48,2304]{3,2,1,0:T(8,128)(2,1)S(1)} %fusion.70), channel_id=1, source_target_pairs={{0,4},{2,6},{4,0},{6,2},{8,12},{10,14},{12,8},{14,10},{16,20},{18,... | collective-permute-start | bytes 2654216 | tf_op jit(solution)/shard_map/ppermute | solution.py:201
  531.2 25.6 %collective-permute-start.39 = (bf16[2,2,192,768]{3,2,1,0:T(8,128)(2,1)S(1)}, bf16[2,2,192,768]{3,2,1,0:T(8,128)(2,1)S(1)}, u32[]{:S(2)}, u32[]{:S(2)}) collective-permute-start(bf16[2,2,192,768]{3,2,1,0:T(8,128)(2,1)S(1)} %fusion.55), channel_id=1, source_target_pairs={{0,4},{2,6},{4,0},{6,2},{8,12},{10,14},{12,8},{14,10},{16,20},{18,... | collective-permute-start | bytes 3538952 | tf_op jit(solution)/shard_map/ppermute | solution.py:201
  536.9 24.5 %collective-permute-start.31 = (bf16[2,2,48,3072]{3,2,1,0:T(8,128)(2,1)S(1)}, bf16[2,2,48,3072]{3,2,1,0:T(8,128)(2,1)S(1)}, u32[]{:S(2)}, u32[]{:S(2)}) collective-permute-start(bf16[2,2,48,3072]{3,2,1,0:T(8,128)(2,1)S(1)} %fusion.57), channel_id=1, source_target_pairs={{0,2},{2,0},{4,6},{6,4},{8,10},{10,8},{12,14},{14,12},{16,18},{18,... | collective-permute-start | bytes 3538952 | tf_op jit(solution)/shard_map/ppermute | solution.py:201
  540.6 45.0 %collective-permute-start.21 = (bf16[48,2304]{1,0:T(8,128)(2,1)S(1)}, bf16[48,2304]{1,0:T(8,128)(2,1)S(1)}, u32[]{:S(2)}, u32[]{:S(2)}) collective-permute-start(bf16[48,2304]{1,0:T(8,128)(2,1)S(1)} %fusion.132), channel_id=1, source_target_pairs={{1,17},{3,19},{5,21},{7,23},{9,25},{11,27},{13,29},{15,31},{17,1},... | collective-permute-start | bytes 663560 | tf_op jit(solution)/shard_map/ppermute | solution.py:201
  542.8 22.6 %collective-permute-start.36 = (bf16[2,48,3072]{2,1,0:T(8,128)(2,1)S(1)}, bf16[2,48,3072]{2,1,0:T(8,128)(2,1)S(1)}, u32[]{:S(2)}, u32[]{:S(2)}) collective-permute-start(bf16[2,48,3072]{2,1,0:T(8,128)(2,1)S(1)} %fusion.101), channel_id=1, source_target_pairs={{1,9},{3,11},{5,13},{7,15},{9,1},{11,3},{13,5},{15,7},{17,25},{19,... | collective-permute-start | bytes 1769480 | tf_op jit(solution)/shard_map/ppermute | solution.py:201
  544.7 45.2 %collective-permute-start.45 = (bf16[192,768]{1,0:T(8,128)(2,1)S(1)}, bf16[192,768]{1,0:T(8,128)(2,1)S(1)}, u32[]{:S(2)}, u32[]{:S(2)}) collective-permute-start(bf16[192,768]{1,0:T(8,128)(2,1)S(1)} %fusion.118), channel_id=1, source_target_pairs={{1,17},{3,19},{5,21},{7,23},{9,25},{11,27},{13,29},{15,31},{17,1},... | collective-permute-start | bytes 884744 | tf_op jit(solution)/shard_map/ppermute | solution.py:201
  556.9 12.9 %collective-permute-start.16 = (bf16[2,48,2304]{2,1,0:T(8,128)(2,1)S(1)}, bf16[2,48,2304]{2,1,0:T(8,128)(2,1)S(1)}, u32[]{:S(2)}, u32[]{:S(2)}) collective-permute-start(bf16[2,48,2304]{2,1,0:T(8,128)(2,1)S(1)} %fusion.108), channel_id=1, source_target_pairs={{0,8},{2,10},{4,12},{6,14},{8,0},{10,2},{12,4},{14,6},{16,24},{18,... | collective-permute-start | bytes 1327112 | tf_op jit(solution)/shard_map/ppermute | solution.py:201
  561.4 12.0 %collective-permute-start.40 = (bf16[2,192,768]{2,1,0:T(8,128)(2,1)S(1)}, bf16[2,192,768]{2,1,0:T(8,128)(2,1)S(1)}, u32[]{:S(2)}, u32[]{:S(2)}) collective-permute-start(bf16[2,192,768]{2,1,0:T(8,128)(2,1)S(1)} %fusion.100), channel_id=1, source_target_pairs={{0,8},{2,10},{4,12},{6,14},{8,0},{10,2},{12,4},{14,6},{16,24},{18,... | collective-permute-start | bytes 1769480 | tf_op jit(solution)/shard_map/ppermute | solution.py:201
  565.4 14.3 %collective-permute-start.32 = (bf16[2,48,3072]{2,1,0:T(8,128)(2,1)S(1)}, bf16[2,48,3072]{2,1,0:T(8,128)(2,1)S(1)}, u32[]{:S(2)}, u32[]{:S(2)}) collective-permute-start(bf16[2,48,3072]{2,1,0:T(8,128)(2,1)S(1)} %fusion.102), channel_id=1, source_target_pairs={{0,8},{2,10},{4,12},{6,14},{8,0},{10,2},{12,4},{14,6},{16,24},{18,... | collective-permute-start | bytes 1769480 | tf_op jit(solution)/shard_map/ppermute | solution.py:201
  569.8 24.9 %collective-permute-start.37 = (bf16[48,3072]{1,0:T(8,128)(2,1)S(1)}, bf16[48,3072]{1,0:T(8,128)(2,1)S(1)}, u32[]{:S(2)}, u32[]{:S(2)}) collective-permute-start(bf16[48,3072]{1,0:T(8,128)(2,1)S(1)} %fusion.124), channel_id=1, source_target_pairs={{1,17},{3,19},{5,21},{7,23},{9,25},{11,27},{13,29},{15,31},{17,1},... | collective-permute-start | bytes 884744 | tf_op jit(solution)/shard_map/ppermute | solution.py:201
  573.4 14.2 %collective-permute-start.17 = (bf16[48,2304]{1,0:T(8,128)(2,1)S(1)}, bf16[48,2304]{1,0:T(8,128)(2,1)S(1)}, u32[]{:S(2)}, u32[]{:S(2)}) collective-permute-start(bf16[48,2304]{1,0:T(8,128)(2,1)S(1)} %fusion.136), channel_id=1, source_target_pairs={{0,16},{2,18},{4,20},{6,22},{8,24},{10,26},{12,28},{14,30},{16,0},... | collective-permute-start | bytes 663560 | tf_op jit(solution)/shard_map/ppermute | solution.py:201
  579.7 12.7 %collective-permute-start.41 = (bf16[192,768]{1,0:T(8,128)(2,1)S(1)}, bf16[192,768]{1,0:T(8,128)(2,1)S(1)}, u32[]{:S(2)}, u32[]{:S(2)}) collective-permute-start(bf16[192,768]{1,0:T(8,128)(2,1)S(1)} %fusion.122), channel_id=1, source_target_pairs={{0,16},{2,18},{4,20},{6,22},{8,24},{10,26},{12,28},{14,30},{16,0},... | collective-permute-start | bytes 884744 | tf_op jit(solution)/shard_map/ppermute | solution.py:201
  585.7 13.0 %collective-permute-start.33 = (bf16[48,3072]{1,0:T(8,128)(2,1)S(1)}, bf16[48,3072]{1,0:T(8,128)(2,1)S(1)}, u32[]{:S(2)}, u32[]{:S(2)}) collective-permute-start(bf16[48,3072]{1,0:T(8,128)(2,1)S(1)} %fusion.128), channel_id=1, source_target_pairs={{0,16},{2,18},{4,20},{6,22},{8,24},{10,26},{12,28},{14,30},{16,0},... | collective-permute-start | bytes 884744 | tf_op jit(solution)/shard_map/ppermute | solution.py:201
  (108 other events, 649.0 us)
